TPU v7x, 32 devices: a whole 2x2x4 slice. The times are simulated.
32 devices in a mesh: stream: 2 (over core), dp: 16 (over z, y, x).
Axes of the slice: x: 2, y: 2, z: 4, core: 2. Of those that a mesh axis runs over, the one named last changes fastest.
Arguments:
- frames: bfloat16 [256, 13, 13, 512], P(('stream', 'dp')), parts along dimension 0, may hold values from -6 to 6
- cotangent: bfloat16 [256, 13, 13, 512], P(('stream', 'dp')), parts along dimension 0, may hold values from -6 to 6
- clip_counts: int32 [64], P(('stream', 'dp')), parts along dimension 0, may hold values from 0 to 4, as said below
- conv4_weight: float32 [9216, 512], P(('stream', 'dp')), parts along dimension 0, may hold values from -0.09375 to 0.09375
- conv5_weight: float32 [9216, 512], P(('stream', 'dp')), parts along dimension 0, may hold values from -0.09375 to 0.09375
- biases: float32 [1024, 2], P(('stream', 'dp')), parts along dimension 0, may hold values from -1.5 to 1.5
- conv4_momentum: float32 [9216, 512], P(('stream', 'dp')), parts along dimension 0, may hold values from -4429.9605 to 4429.9605
- conv5_momentum: float32 [9216, 512], P(('stream', 'dp')), parts along dimension 0, may hold values from -4429.9605 to 4429.9605
- bias_momentum: float32 [1024, 2], P(('stream', 'dp')), parts along dimension 0, may hold values from -384 to 384
Outputs:
- outputs: bfloat16 [256, 13, 13, 512], P(('stream', 'dp')), parts along dimension 0
- input_grad: bfloat16 [256, 13, 13, 512], P(('stream', 'dp')), parts along dimension 0
- conv4_moment: float32 [9216, 512], P(('stream', 'dp')), parts along dimension 0
- conv5_moment: float32 [9216, 512], P(('stream', 'dp')), parts along dimension 0
- conv4_new: float32 [9216, 512], P(('stream', 'dp')), parts along dimension 0
- conv5_new: float32 [9216, 512], P(('stream', 'dp')), parts along dimension 0
- conv4_copy: bfloat16 [9216, 512], P(('stream', 'dp')), parts along dimension 0
- conv5_copy: bfloat16 [9216, 512], P(('stream', 'dp')), parts along dimension 0
- bias_moment: float32 [1024, 2], P(('stream', 'dp')), parts along dimension 0
- bias_new: float32 [1024, 2], P(('stream', 'dp')), parts along dimension 0
There are 2 independent parts, one for each index of `stream`. A program takes and returns all parts, laid end to end along the dimension named above; each array names one. Nothing has to cross between parts.
Inputs may be any that keep to these rules, and one draw needn't show every extreme that they name: `clip_counts`: device d of dp holds video slots 2d and 2d + 1; its frame slots hold the first video's clips, then the second's, then empty slots. The two counts of one device sum to at most 8, and some device is full; 0 is an empty video slot.
All inputs are finite; a program needn't handle non-finite values.
Results may differ from a plain program's by a relative error of at most 0.0083.
Values may be sent and summed in bfloat16 or wider, within the bound.
No kernel may reach another device: no remote copies, remote signals or barrier semaphores. Data moves between devices by JAX's collectives and lax.ppermute only.
A program may use at most 256 MiB of HBM per device.

v0:
```python
import jax
import jax.numpy as jnp
from jax import lax
from jax.sharding import PartitionSpec as P

NS_STEPS = 5


def activate(value):
    return jax.nn.gelu(value, approximate=True)


def patches(field):
    count, side = (field.shape[0], field.shape[1])
    padded = jnp.pad(field, ((0, 0), (1, 1), (1, 1), (0, 0)))
    taps = [padded[:, r : r + side, s : s + side, :] for r in range(3) for s in range(3)]
    return jnp.concatenate(taps, axis=-1).reshape(count * side * side, -1)


def fold_taps(grads, count, side, width):
    pieces = grads.reshape(count, side, side, 9, width)
    padded = jnp.zeros((count, side + 2, side + 2, width), jnp.float32)
    for r in range(3):
        for s in range(3):
            padded = padded.at[:, r : r + side, s : s + side, :].add(pieces[:, :, :, 3 * r + s, :])
    return padded[:, 1 : side + 1, 1 : side + 1, :]


def contract_rows(left, right):
    return lax.dot_general(
        left, right, (((0,), (0,)), ((), ())), preferred_element_type=jnp.float32
    )


def times_transposed(left, right):
    return lax.dot_general(
        left, right, (((1,), (1,)), ((), ())), preferred_element_type=jnp.float32
    )


def gram_of(iterate):
    return lax.dot_general(
        iterate, iterate, (((0,), (0,)), ((), ())), precision=lax.Precision.HIGHEST
    )


def newton_step(iterate, gram):
    poly = -4.775 * gram + 2.0315 * jnp.dot(gram, gram, precision=lax.Precision.HIGHEST)
    return 3.4445 * iterate + jnp.dot(iterate, poly, precision=lax.Precision.HIGHEST)


def on_device(
    frames,
    cotangent,
    clip_counts,
    conv4_weight,
    conv5_weight,
    biases,
    conv4_momentum,
    conv5_momentum,
    bias_momentum,
):
    count, side, width = (frames.shape[0], frames.shape[1], frames.shape[3])
    low4, low5, low_bias = (
        lax.all_gather(conv4_weight.astype(jnp.bfloat16), "dp", axis=0, tiled=True),
        lax.all_gather(conv5_weight.astype(jnp.bfloat16), "dp", axis=0, tiled=True),
        lax.all_gather(biases.astype(jnp.bfloat16), "dp", axis=0, tiled=True),
    )
    bias_full = low_bias.astype(jnp.float32)
    patch_in = patches(frames)
    first = jnp.dot(patch_in, low4, preferred_element_type=jnp.float32) + bias_full[:, 0]
    hidden, pull_first = jax.vjp(activate, first)
    hidden = hidden.astype(jnp.bfloat16)
    patch_mid = patches(hidden.reshape(count, side, side, width))
    second = jnp.dot(patch_mid, low5, preferred_element_type=jnp.float32) + bias_full[:, 1]
    result, pull_second = jax.vjp(activate, second)
    outputs = result.astype(jnp.bfloat16).reshape(count, side, side, width)
    live = jnp.sum(clip_counts)
    mask = (jnp.arange(count, dtype=jnp.int32) < live).astype(jnp.float32)
    upstream = (cotangent.astype(jnp.float32) * mask[:, None, None, None]).reshape(
        count * side * side, width
    )
    delta_second = pull_second(upstream)[0].astype(jnp.bfloat16)
    back_mid = fold_taps(times_transposed(delta_second, low5), count, side, width)
    delta_first = pull_first(back_mid.reshape(count * side * side, width))[0].astype(jnp.bfloat16)
    back_in = fold_taps(times_transposed(delta_first, low4), count, side, width)
    input_grad = back_in.astype(jnp.bfloat16)
    bias_terms = jnp.stack(
        [
            jnp.sum(delta_first.astype(jnp.float32), axis=0),
            jnp.sum(delta_second.astype(jnp.float32), axis=0),
        ],
        axis=1,
    )
    whole5 = contract_rows(patch_mid, delta_second)
    whole4 = contract_rows(patch_in, delta_first)
    grad5, grad4, grad_bias = (
        lax.psum_scatter(whole5, "dp", scatter_dimension=0, tiled=True),
        lax.psum_scatter(whole4, "dp", scatter_dimension=0, tiled=True),
        lax.psum_scatter(bias_terms, "dp", scatter_dimension=0, tiled=True),
    )
    moment4 = 0.5 * conv4_momentum + grad4
    moment5 = 0.5 * conv5_momentum + grad5
    update4 = grad4 + 0.5 * moment4
    update5 = grad5 + 0.5 * moment5
    square4, square5 = lax.psum((jnp.sum(update4 * update4), jnp.sum(update5 * update5)), "dp")
    iterate4 = update4 / (jnp.sqrt(square4) + 1e-07)
    iterate5 = update5 / (jnp.sqrt(square5) + 1e-07)
    for step in range(NS_STEPS):
        gram4, gram5 = lax.psum((gram_of(iterate4), gram_of(iterate5)), "dp")
        iterate4 = newton_step(iterate4, gram4)
        iterate5 = newton_step(iterate5, gram5)
    new4 = conv4_weight - iterate4
    new5 = conv5_weight - iterate5
    bias_moment = 0.5 * bias_momentum + grad_bias
    bias_new = biases - 0.001 * (grad_bias + 0.5 * bias_moment)
    return (
        outputs,
        input_grad,
        moment4,
        moment5,
        new4,
        new5,
        new4.astype(jnp.bfloat16),
        new5.astype(jnp.bfloat16),
        bias_moment,
        bias_new,
    )


def solution(mesh):
    in_specs = (
        P(("stream", "dp"), None, None, None),
        P(("stream", "dp"), None, None, None),
        P(("stream", "dp")),
        P(("stream", "dp"), None),
        P(("stream", "dp"), None),
        P(("stream", "dp"), None),
        P(("stream", "dp"), None),
        P(("stream", "dp"), None),
        P(("stream", "dp"), None),
    )
    out_specs = (
        P(("stream", "dp"), None, None, None),
        P(("stream", "dp"), None, None, None),
        P(("stream", "dp"), None),
        P(("stream", "dp"), None),
        P(("stream", "dp"), None),
        P(("stream", "dp"), None),
        P(("stream", "dp"), None),
        P(("stream", "dp"), None),
        P(("stream", "dp"), None),
        P(("stream", "dp"), None),
    )
    return jax.shard_map(
        on_device, mesh=mesh, in_specs=in_specs, out_specs=out_specs, check_vma=False
    )
```

profile of v0, /device:TPU:0, one launch (start us, length us, event | category | flops | bytes accessed | tf_op | source)
XLA Modules:
  0.0 1371.5 jit_solution(1059627762561086060)
XLA Ops:
  11.8 42.4 %all-gather = bf16[16,32,2]{1,2,0:T(2,128)(2,1)S(1)} all-gather(bf16[1,32,2]{1,2,0:T(2,128)(2,1)S(1)} %convert_bitcast_fusion), channel_id=1, replica_groups=mesh['stream'=2,'dp'=16] {'dp'}, dimensions={0}, use_global_device_ids=true | all-gather | bytes 2176 | tf_op jit(solution)/shard_map/all_gather | solution.py:67
  56.7 3.4 copy.322
  60.1 4.7 reshape.779
  65.7 11.1 copy.320
  76.8 16.5 %reshape.776 = bf16[1352,4608]{1,0:T(8,128)(2,1)} reshape(bf16[8,13,13,4608]{3,2,1,0:T(8,128)(2,1)} %copy.320) | data formatting | bytes 24920064 | tf_op jit(solution)/shard_map/reshape | solution.py:17
  94.6 12.7 multiply_convert_fusion.1
  110.0 9.8 pad_slice_fusion.8
  119.8 3.4 concatenate.75
  123.3 3.4 concatenate.69
  126.7 3.4 concatenate.70
  130.1 3.4 concatenate.71
  133.5 3.4 concatenate.72
  136.9 3.4 concatenate.73
  143.5 2.7 constant_dynamic-update-slice_fusion.9
  156.1 20.8 %all-gather.6.cloned.1.call-done = bf16[4608,512]{1,0:T(8,128)(2,1)} async-done(((bf16[288,512]{1,0:T(8,128)(2,1)}), bf16[4608,512]{1,0:T(8,128)(2,1)}) %all-gather.6.cloned.1.call-update) | async-done | bytes 4718608 | tf_op jit(solution)/shard_map/all_gather | solution.py:66
  176.9 14.4 %convert_reduce_fusion = (f32[512]{0:T(512)}, bf16[1352,512]{1,0:T(8,128)(2,1)S(1)}, bf16[1352,512]{1,0:T(8,128)(2,1)}) fusion(f32[1352,512]{1,0:T(8,128)S(1)} %copy-done.31, f32[512]{0:T(512)S(1)} %bitcast.141, bf16[1352,4608]{1,0:T(8,128)(2,1)} %constant_dynamic-update-slice_fusion.1, bf16[4608,512]{1,0:T(8,128)(2,1)} %all-gather.6.cloned.1.call-done), kind=kOutput, calls=%fused_computation.63 | convolution fusion | flops 6396841472 | bytes 22720512 | tf_op jit(solution)/shard_map/dot_general | solution.py:75
  192.4 12.7 fusion.65
  207.0 14.1 %fusion.62 = f32[1352,4608]{1,0:T(8,128)} fusion(bf16[1352,512]{1,0:T(8,128)(2,1)S(1)} %copy-done.46, bf16[4608,512]{1,0:T(8,128)(2,1)} %all-gather.6.cloned.1.call-done), kind=kOutput, calls=%fused_computation.159 | convolution fusion | flops 6379536384 | bytes 31023104 | tf_op jit(solution)/shard_map/dot_general | solution.py:36
  221.1 31.2 %reshape.780 = f32[8,13,13,9,512]{4,3,2,1,0:T(8,128)} reshape(f32[1352,4608]{1,0:T(8,128)} %fusion.62) | data formatting | bytes 49840128 | tf_op jit(solution)/shard_map/reshape | solution.py:21
  252.3 72.8 %fusion.56 = (f32[8,13,13,1,512]{4,3,2,1,0:T(1,128)S(1)}, f32[8,13,13,1,512]{4,3,2,1,0:T(1,128)}, f32[8,13,13,1,512]{4,3,2,1,0:T(1,128)}, f32[8,13,13,1,512]{4,3...) fusion(f32[8,13,13,9,512]{4,3,2,1,0:T(8,128)} %reshape.780), kind=kLoop, calls=%fused_computation.153 | loop fusion | bytes 49840128 | tf_op jit(solution)/shard_map/slice | solution.py:25
  329.1 2.3 fusion.30
  331.4 2.9 fusion.14
  346.8 3.7 convert_reduce_fusion.1
  350.5 13.1 fusion.64
  363.8 11.1 reduce-scatter.8.cloned.1.call-done
  376.7 174.6 %reduce-scatter.6.cloned.1.call-done = f32[288,512]{1,0:T(8,128)} async-done(((f32[4608,512]{1,0:T(8,128)}), f32[288,512]{1,0:T(8,128)}) %reduce-scatter.6.cloned.1.call-update) | async-done | bytes 589840 | tf_op jit(solution)/shard_map/reduce_scatter | solution.py:99
  553.1 40.3 %all-reduce.4 = (f32[]{:T(128)}, f32[]{:T(128)}) all-reduce(f32[]{:T(128)} %get-tuple-element.376, f32[]{:T(128)} %get-tuple-element.374), channel_id=1, replica_groups=mesh['stream'=2,'dp'=16] {'dp'}, use_global_device_ids=true, to_apply=%region_5.6 | all-reduce | flops 2 | bytes 16 | tf_op jit(solution)/shard_map/psum | solution.py:106
  594.8 4.2 fusion.51
  599.0 4.1 fusion.52
  603.4 122.2 %all-reduce.24.cloned.1.call-done = (f32[512,512]{1,0:T(8,128)}, f32[512,512]{1,0:T(8,128)}) async-done(((f32[512,512]{1,0:T(8,128)}, f32[512,512]{1,0:T(8,128)}), (f32[512,512]{1,0:T(8,128)}, f32[512,512]{1,0:T(8,128)})) %all-reduce.24.cloned.1.call-update) | async-done | bytes 2097168 | tf_op jit(solution)/shard_map/psum | solution.py:110
  725.5 3.9 fusion.48
  730.7 2.8 fusion.66
  736.7 2.8 fusion.70
  739.8 125.6 %all-reduce.22.cloned.1.call-done = (f32[512,512]{1,0:T(8,128)}, f32[512,512]{1,0:T(8,128)}) async-done(((f32[512,512]{1,0:T(8,128)}, f32[512,512]{1,0:T(8,128)}), (f32[512,512]{1,0:T(8,128)}, f32[512,512]{1,0:T(8,128)})) %all-reduce.22.cloned.1.call-update) | async-done | bytes 2097168 | tf_op jit(solution)/shard_map/psum | solution.py:110
  865.5 4.0 fusion.47
  870.6 2.8 fusion.67
  876.5 2.9 fusion.71
  879.9 14.0 %fusion.63 = f32[1352,4608]{1,0:T(8,128)} fusion(bf16[1352,512]{1,0:T(8,128)(2,1)S(1)} %get-tuple-element.371, bf16[4608,512]{1,0:T(8,128)(2,1)} %all-gather.4.cloned.1.call-done), kind=kOutput, calls=%fused_computation.160 | convolution fusion | flops 6379536384 | bytes 31023104 | tf_op jit(solution)/shard_map/dot_general | solution.py:36
  893.9 30.8 %reshape.794 = f32[8,13,13,9,512]{4,3,2,1,0:T(8,128)} reshape(f32[1352,4608]{1,0:T(8,128)} %fusion.63) | data formatting | bytes 49840128 | tf_op jit(solution)/shard_map/reshape | solution.py:21
  924.7 80.5 %all-reduce.20.cloned.1.call-done = (f32[512,512]{1,0:T(8,128)}, f32[512,512]{1,0:T(8,128)}) async-done(((f32[512,512]{1,0:T(8,128)}, f32[512,512]{1,0:T(8,128)}), (f32[512,512]{1,0:T(8,128)}, f32[512,512]{1,0:T(8,128)})) %all-reduce.20.cloned.1.call-update) | async-done | bytes 2097168 | tf_op jit(solution)/shard_map/psum | solution.py:110
  1005.3 3.9 fusion.46
  1010.4 2.8 fusion.68
  1017.1 2.9 fusion.72
  1020.0 71.1 %fusion.55 = (f32[8,13,13,1,512]{4,3,2,1,0:T(1,128)S(1)}, f32[8,13,13,1,512]{4,3,2,1,0:T(1,128)}, f32[8,13,13,1,512]{4,3,2,1,0:T(1,128)}, f32[8,13,13,1,512]{4,3...) fusion(f32[8,13,13,9,512]{4,3,2,1,0:T(8,128)} %reshape.794), kind=kLoop, calls=%fused_computation.152 | loop fusion | bytes 49840128 | tf_op jit(solution)/shard_map/slice | solution.py:25
  1094.2 2.2 scatter-add.75
  1096.6 6.3 fusion.29
  1102.8 6.1 fusion.15
  1109.0 4.0 fusion.21
  1113.0 32.9 %all-reduce.18.cloned.1.call-done = (f32[512,512]{1,0:T(8,128)}, f32[512,512]{1,0:T(8,128)}) async-done(((f32[512,512]{1,0:T(8,128)}, f32[512,512]{1,0:T(8,128)}), (f32[512,512]{1,0:T(8,128)}, f32[512,512]{1,0:T(8,128)})) %all-reduce.18.cloned.1.call-update) | async-done | bytes 2097168 | tf_op jit(solution)/shard_map/psum | solution.py:110
  1145.8 4.0 fusion.45
  1151.8 2.9 fusion.69
  1157.8 2.9 fusion.73
  1160.7 4.8 fusion.20
  1165.5 3.5 reshape.778
  1169.0 3.6 copy.342
  1172.7 4.1 fusion.19
  1176.8 4.1 fusion.18
  1180.9 4.0 fusion.17
  1184.9 3.9 fusion.16
  1188.8 3.1 slice.871
  1191.9 32.2 %reduce-scatter.10.cloned.1.call-done = f32[32,2]{1,0:T(8,128)} async-done(((f32[512,2]{1,0:T(8,128)}), f32[32,2]{1,0:T(8,128)}) %reduce-scatter.10.cloned.1.call-update) | async-done | bytes 272
  1225.5 127.7 %all-reduce.16.cloned.1.call-done = (f32[512,512]{1,0:T(8,128)}, f32[512,512]{1,0:T(8,128)}) async-done(((f32[512,512]{1,0:T(8,128)}, f32[512,512]{1,0:T(8,128)}), (f32[512,512]{1,0:T(8,128)}, f32[512,512]{1,0:T(8,128)})) %all-reduce.16.cloned.1.call-update) | async-done | bytes 2097168 | tf_op jit(solution)/shard_map/psum | solution.py:110
  1353.2 4.1 fusion.44
  1357.3 3.2 fusion.60
  (181 shorter events, 76.3 us)
Async XLA Ops:
  7.2 49.1 %copy-start.33 = (bf16[8,13,13,512]{3,0,2,1:T(8,128)(2,1)S(1)}, bf16[8,13,13,512]{3,0,2,1:T(8,128)(2,1)}, u32[]{:S(2)}) copy-start(bf16[8,13,13,512]{3,0,2,1:T(8,128)(2,1)} %param.46) | copy-start | bytes 4153348
  7.2 87.4 %all-gather.4.cloned.1.call-start = ((), (), s32[]{:S(2)}) async-start(), calls=%async_computation.3 | async-start | bytes 5013504 | tf_op jit(solution)/shard_map/all_gather | solution.py:65
  9.2 167.7 %all-gather.6.cloned.1.call-start = ((), (), s32[]{:S(2)}) async-start(), calls=%async_computation.4 | async-start | bytes 5013504 | tf_op jit(solution)/shard_map/all_gather | solution.py:66
  11.1 363.8 %reduce-scatter.8.cloned.1.call-start = ((), (), s32[]{:S(2)}) async-start(), calls=%async_computation.6 | async-start | bytes 10027008 | tf_op jit(solution)/shard_map/reduce_scatter | solution.py:98
  60.1 4.7 copy-start
  107.3 1.1 copy-start.17
  142.0 4.2 copy-start.25
  143.5 3.9 copy-start.24
  146.2 2.4 copy-start.23
  147.4 2.4 copy-start.18
  148.6 2.5 copy-start.22
  149.9 2.5 copy-start.21
  151.2 2.5 copy-start.20
  152.4 2.5 copy-start.19
  153.7 23.2 %copy-start.31 = (f32[1352,512]{1,0:T(8,128)S(1)}, f32[1352,512]{1,0:T(8,128)}, u32[]{:S(2)}) copy-start(f32[1352,512]{1,0:T(8,128)} %reshape.779) | copy-start | bytes 8306692
  191.3 1.1 copy-start.45
  205.1 1.3 copy-start.44
  205.1 1.9 copy-start.46
  205.1 346.2 %reduce-scatter.6.cloned.1.call-start = ((), (), s32[]{:S(2)}) async-start(), calls=%async_computation.5 | async-start | bytes 10027008 | tf_op jit(solution)/shard_map/reduce_scatter | solution.py:99
  327.2 1.8 copy-start.12
  329.1 2.3 copy-start.11
  331.4 2.9 copy-start.10
  334.3 1.8 copy-start.9
  336.1 1.8 copy-start.8
  337.9 1.8 copy-start.7
  339.7 1.8 copy-start.6
  363.7 11.2 copy-start.34
  363.7 187.6 %copy-start.35 = (f32[288,512]{1,0:T(8,128)S(1)}, f32[288,512]{1,0:T(8,128)}, u32[]{:S(2)}) copy-start(f32[288,512]{1,0:T(8,128)} %param.51) | copy-start | bytes 1769476
  363.7 361.8 %all-reduce.24.cloned.1.call-start = ((), (), s32[]{:S(2)}) async-start(), calls=%async_computation.12 | async-start | bytes 4194304 | tf_op jit(solution)/shard_map/psum | solution.py:110
  376.7 226.4 %copy-start.36 = (f32[288,512]{1,0:T(8,128)}, f32[288,512]{1,0:T(8,128)S(1)}, u32[]{:S(2)}) copy-start(f32[288,512]{1,0:T(8,128)S(1)} %get-tuple-element.375) | copy-start | bytes 1769476
  553.1 176.3 %copy-start.38 = (f32[288,512]{1,0:T(8,128)}, f32[288,512]{1,0:T(8,128)S(1)}, u32[]{:S(2)}) copy-start(f32[288,512]{1,0:T(8,128)S(1)} %get-tuple-element.377) | copy-start | bytes 1769476
  603.1 126.4 %copy-start.40 = (f32[288,512]{1,0:T(8,128)S(1)}, f32[288,512]{1,0:T(8,128)}, u32[]{:S(2)}) copy-start(f32[288,512]{1,0:T(8,128)} %reduce-scatter.6.cloned.1.call-done) | copy-start | bytes 1769476
  603.1 262.3 %all-reduce.22.cloned.1.call-start = ((), (), s32[]{:S(2)}) async-start(), calls=%async_computation.11 | async-start | bytes 4194304 | tf_op jit(solution)/shard_map/psum | solution.py:110
  729.5 4.1 copy-start.29
  730.7 4.7 copy-start.37
  730.7 4.7 copy-start.39
  739.6 265.7 %all-reduce.20.cloned.1.call-start = ((), (), s32[]{:S(2)}) async-start(), calls=%async_computation.10 | async-start | bytes 4194304 | tf_op jit(solution)/shard_map/psum | solution.py:110
  869.4 4.0 copy-start.30
  879.4 266.5 %all-reduce.18.cloned.1.call-start = ((), (), s32[]{:S(2)}) async-start(), calls=%async_computation.9 | async-start | bytes 4194304 | tf_op jit(solution)/shard_map/psum | solution.py:110
  1009.2 4.0 copy-start.28
  1016.3 0.8 copy-start.13
  1020.0 71.2 %copy-start.41 = (f32[512]{0:T(512)S(1)}, f32[512]{0:T(512)}, u32[]{:S(2)}) copy-start(f32[512]{0:T(512)} %get-tuple-element.372) | copy-start | bytes 6148
  1020.0 204.2 %reduce-scatter.10.cloned.1.call-start = ((), (), s32[]{:S(2)}) async-start(), calls=%async_computation.7 | async-start | bytes 278528
  1096.3 256.8 %all-reduce.16.cloned.1.call-start = ((), (), s32[]{:S(2)}) async-start(), calls=%async_computation.8 | async-start | bytes 4194304 | tf_op jit(solution)/shard_map/psum | solution.py:110
  1096.6 6.3 copy-start.5
  1102.8 6.1 copy-start.4
  1149.8 4.9 copy-start.26
  1151.0 0.8 copy-start.15
  1151.8 4.8 copy-start.14
  1169.0 3.6 copy-start.3
  1172.7 4.1 copy-start.2
  1176.8 4.1 copy-start.1
  1188.8 36.1 %copy-start.42 = (f32[32,2]{0,1:T(2,128)S(1)}, f32[32,2]{0,1:T(2,128)}, u32[]{:S(2)}) copy-start(f32[32,2]{0,1:T(2,128)} %param.50) | copy-start | bytes 772
  1188.8 36.1 %copy-start.43 = (f32[32,2]{0,1:T(2,128)S(1)}, f32[32,2]{0,1:T(2,128)}, u32[]{:S(2)}) copy-start(f32[32,2]{0,1:T(2,128)} %param.53) | copy-start | bytes 772
  1188.8 168.4 %copy-start.16 = (f32[288,512]{1,0:T(8,128)S(1)}, f32[288,512]{1,0:T(8,128)}, u32[]{:S(2)}) copy-start(f32[288,512]{1,0:T(8,128)} %copy-done.15) | copy-start | bytes 1769476
  1353.2 7.3 copy-start.27
  1357.3 5.1 copy-start.32
Sparse Core Ops, SparseCore 0:
  11.4 83.1 all-gather.3
  98.0 78.8 all-gather.5
  205.2 169.5 reduce-scatter.7
  381.4 169.8 reduce-scatter.5
  603.3 122.2 all-reduce.23
  739.7 125.7 all-reduce.21
  879.5 125.7 all-reduce.19
  1020.1 125.7 all-reduce.17
  1148.7 75.4 reduce-scatter.9
  1230.4 122.6 all-reduce.15
where the time goes:
time: 1380 us; the launch traced here: 1370 us
  waiting for transfers between devices  729 us (53%)
  local copies, waits for them, and re-layouts  324 us (23%)
  matrix products  156 us (11%)
  blocking collectives  82.7 us (6%)
  other arithmetic  62.4 us (5%)
  between operations  16.4 us (1%)
    psum x5, waiting for transfers between devices, on_device(): gram4, gram5 = lax.psum((gram_of(iterate4), gram_of(iterate5)), 'dp')  489 us
    reduce_scatter x1, waiting for transfers between devices, on_device(): lax.psum_scatter(whole4, 'dp', scatter_dimension=0, tiled=True)  175 us
    slice x3, local copies, waits for them, and re-layouts, fold_taps(): pieces[:, :, :, 3 * r + s, :]  146 us
    reshape x2, local copies, waits for them, and re-layouts, fold_taps(): pieces = grads.reshape(count, side, side, 9, width)  62 us
    scatter-add x16, other arithmetic, fold_taps(): padded.at[:, r:r + side, s:s + side, :].add(pieces[:, :, :, 3 * r + s, :])  46.8 us
    all_gather x1, blocking collectives, on_device(): lax.all_gather(biases.astype(jnp.bfloat16), 'dp', axis=0, tiled=True)  42.4 us
    psum x1, blocking collectives, on_device(): lax.psum((jnp.sum(update4 * update4), jnp.sum(update5 * update5)), 'dp')  40.3 us
    concatenate x11, local copies, waits for them, and re-layouts, patches(): return jnp.concatenate(taps, axis=-1).reshape(count * side * side, -1)  36.1 us
  transfers between devices with their start and end apart: 10, of which 10 were waited for; matrix products, arithmetic and copies ran while one was open for 32% of the time, Pallas kernels for 0%

commit v1 on v0

v1 whole, which is shorter than its diff:
```python
import functools
import math

import jax
import jax.numpy as jnp
from jax import lax
from jax.experimental import pallas as pl
from jax.experimental.pallas import tpu as pltpu
from jax.sharding import PartitionSpec as P

NS_STEPS = 5
BF = jnp.bfloat16
F32 = jnp.float32


def split_three(n):
    c = max(d for d in range(1, n + 1) if n % d == 0 and d**3 <= n)
    rest = n // c
    b = max(d for d in range(1, rest + 1) if rest % d == 0 and d**2 <= rest)
    return rest // b, b, c


def shift_pairs(dims, axis, step):
    pairs = []
    for index in range(math.prod(dims)):
        place = [index // (dims[1] * dims[2]), index // dims[2] % dims[1], index % dims[2]]
        place[axis] = (place[axis] + step) % dims[axis]
        pairs.append((index, (place[0] * dims[1] + place[1]) * dims[2] + place[2]))
    return pairs


class Group:
    def __init__(self, n):
        self.dims = split_three(n)
        me = lax.axis_index("dp")
        self.place = (me // (self.dims[1] * self.dims[2]), me // self.dims[2] % self.dims[1], me % self.dims[2])

    def spread(self, block, axis):
        size = self.dims[axis]
        got = [block]
        for j in range(1, size):
            got.append(lax.ppermute(block, "dp", shift_pairs(self.dims, axis, -j)))
        return jnp.stack(got)

    def settle(self, stack, at, axis):
        return jnp.roll(stack, self.place[axis], axis=at)

    def gather(self, block):
        rows, cols = block.shape
        half = rows // 2
        near = self.spread(block, 0)
        one = self.spread(self.spread(near[:, :half], 2), 1)
        two = self.spread(self.spread(near[:, half:], 1), 2)
        one = jnp.transpose(one, (2, 0, 1, 3, 4))
        two = jnp.transpose(two, (2, 1, 0, 3, 4))
        whole = jnp.concatenate([one, two], axis=3)
        for axis in range(3):
            whole = self.settle(whole, axis, axis)
        return whole.reshape(-1, cols)

    def gather_small(self, block):
        got = self.spread(self.spread(self.spread(block, 0), 1), 2)
        got = jnp.moveaxis(got, (0, 1, 2), (2, 1, 0))
        for axis in range(3):
            got = self.settle(got, axis, axis)
        return got.reshape((-1,) + block.shape[1:])

    def fold(self, parts, at, axis, kind):
        size = self.dims[axis]
        total = lax.dynamic_index_in_dim(parts, self.place[axis], at, keepdims=False)
        for j in range(1, size):
            out = lax.dynamic_index_in_dim(parts, (self.place[axis] + j) % size, at, keepdims=False)
            got = lax.ppermute(out.astype(kind), "dp", shift_pairs(self.dims, axis, j))
            total = total + got.astype(F32)
        return total

    def scatter_sum(self, whole, kind):
        cols = whole.shape[1]
        parts = whole.reshape(self.dims + (-1, cols))
        half = parts.shape[3] // 2
        one = self.fold(self.fold(parts[:, :, :, :half], 2, 2, kind), 1, 1, kind)
        two = self.fold(self.fold(parts[:, :, :, half:], 1, 1, kind), 1, 2, kind)
        return self.fold(jnp.concatenate([one, two], axis=1), 0, 0, kind)

    def scatter_sum_small(self, whole):
        parts = whole.reshape(self.dims + (-1,) + whole.shape[1:])
        return self.fold(self.fold(self.fold(parts, 2, 2, F32), 1, 1, F32), 0, 0, F32)

    def sum_gram(self, gram):
        half = gram.shape[0] // 2
        packed = jnp.concatenate([gram[:half, :half], gram[:half, half:], gram[half:, half:]], axis=0)
        packed = self.gather(self.scatter_sum(packed, F32))
        corner = packed[half : 2 * half]
        return jnp.concatenate(
            [
                jnp.concatenate([packed[:half], corner], axis=1),
                jnp.concatenate([corner.T, packed[2 * half :]], axis=1),
            ],
            axis=0,
        )


def activate(value):
    return jax.nn.gelu(value, approximate=True)


def convolve(field, weight):
    width = field.shape[3]
    return lax.conv_general_dilated(
        field,
        weight.reshape(3, 3, width, -1),
        (1, 1),
        ((1, 1), (1, 1)),
        dimension_numbers=("NHWC", "HWIO", "NHWC"),
        preferred_element_type=F32,
    )


def convolve_back(delta, weight):
    width = delta.shape[3]
    return lax.conv_general_dilated(
        delta,
        weight.reshape(3, 3, -1, width)[::-1, ::-1],
        (1, 1),
        ((1, 1), (1, 1)),
        dimension_numbers=("NHWC", "HWOI", "NHWC"),
        preferred_element_type=F32,
    )


def weight_gradient(field, delta):
    grad = lax.conv_general_dilated(
        field,
        delta,
        (1, 1),
        ((1, 1), (1, 1)),
        dimension_numbers=("CHWN", "IHWO", "HWNC"),
        preferred_element_type=F32,
    )
    return grad.reshape(-1, delta.shape[3])


def halves(value):
    high = value.astype(BF)
    return high, (value - high.astype(F32)).astype(BF)


def product(left, right):
    dot = functools.partial(jnp.dot, preferred_element_type=F32)
    return dot(left[0], right[0]) + (dot(left[0], right[1]) + dot(left[1], right[0]))


def newton_kernel(gram_ref, update_ref, weight_ref, new_ref, copy_ref):
    gram = gram_ref[...]
    size = gram.shape[0]
    diagonal = lax.broadcasted_iota(jnp.int32, (size, size), 0) == lax.broadcasted_iota(jnp.int32, (size, size), 1)
    square = jnp.sum(jnp.where(diagonal, gram, 0.0))
    scale = 1.0 / (jnp.sqrt(square) + 1e-07)
    gram = gram * scale * scale
    iterate = update_ref[...] * scale
    for step in range(NS_STEPS):
        parts = halves(gram)
        poly = halves(-4.775 * gram + 2.0315 * product(parts, parts))
        iterate = 3.4445 * iterate + product(halves(iterate), poly)
        if step < NS_STEPS - 1:
            middle = 3.4445 * gram + product(parts, poly)
            gram = 3.4445 * middle + product(halves(middle), poly)
    new = weight_ref[...] - iterate
    new_ref[...] = new
    copy_ref[...] = new.astype(BF)


def newton(gram, update, weight):
    return pl.pallas_call(
        newton_kernel,
        out_shape=(jax.ShapeDtypeStruct(weight.shape, F32), jax.ShapeDtypeStruct(weight.shape, BF)),
        compiler_params=pltpu.CompilerParams(vmem_limit_bytes=48 * 1024 * 1024),
        cost_estimate=pl.CostEstimate(flops=100 * 512**3, bytes_accessed=4 * 1024 * 1024, transcendentals=0),
    )(gram, update, weight)


def on_device(
    n_dp,
    frames,
    cotangent,
    clip_counts,
    conv4_weight,
    conv5_weight,
    biases,
    conv4_momentum,
    conv5_momentum,
    bias_momentum,
):
    group = Group(n_dp)
    count, width = (frames.shape[0], frames.shape[3])
    half = width // 2
    bias_full = group.gather_small(biases.astype(BF)).astype(F32)
    low4 = conv4_weight.astype(BF)
    low5 = conv5_weight.astype(BF)
    full4 = [group.gather(low4[:, :half]), group.gather(low4[:, half:])]
    full5 = [group.gather(low5[:, :half]), group.gather(low5[:, half:])]

    first = jnp.concatenate([convolve(frames, full) for full in full4], axis=3) + bias_full[:, 0]
    hidden, pull_first = jax.vjp(activate, first)
    hidden = hidden.astype(BF)
    second = jnp.concatenate([convolve(hidden, full) for full in full5], axis=3) + bias_full[:, 1]
    result, pull_second = jax.vjp(activate, second)
    outputs = result.astype(BF)
    live = jnp.sum(clip_counts)
    mask = (jnp.arange(count, dtype=jnp.int32) < live).astype(F32)
    upstream = cotangent.astype(F32) * mask[:, None, None, None]
    delta_second = pull_second(upstream)[0].astype(BF)
    whole5 = weight_gradient(hidden, delta_second)
    grad5 = jnp.concatenate([group.scatter_sum(whole5[:, :half], BF), group.scatter_sum(whole5[:, half:], BF)], axis=1)
    back_mid = convolve_back(delta_second[..., :half], full5[0]) + convolve_back(delta_second[..., half:], full5[1])
    delta_first = pull_first(back_mid)[0].astype(BF)
    whole4 = weight_gradient(frames, delta_first)
    grad4 = jnp.concatenate([group.scatter_sum(whole4[:, :half], BF), group.scatter_sum(whole4[:, half:], BF)], axis=1)
    back_in = convolve_back(delta_first[..., :half], full4[0]) + convolve_back(delta_first[..., half:], full4[1])
    input_grad = back_in.astype(BF)
    bias_terms = jnp.stack(
        [
            jnp.sum(delta_first.astype(F32), axis=(0, 1, 2)),
            jnp.sum(delta_second.astype(F32), axis=(0, 1, 2)),
        ],
        axis=1,
    )
    grad_bias = group.scatter_sum_small(bias_terms)

    moment5 = 0.5 * conv5_momentum + grad5
    update5 = grad5 + 0.5 * moment5
    moment4 = 0.5 * conv4_momentum + grad4
    update4 = grad4 + 0.5 * moment4

    def gram_of(update):
        low = update.astype(BF)
        return lax.dot_general(low, low, (((0,), (0,)), ((), ())), preferred_element_type=F32)

    new5, copy5 = newton(group.sum_gram(gram_of(update5)), update5, conv5_weight)
    new4, copy4 = newton(group.sum_gram(gram_of(update4)), update4, conv4_weight)
    bias_moment = 0.5 * bias_momentum + grad_bias
    bias_new = biases - 0.001 * (grad_bias + 0.5 * bias_moment)
    return (
        outputs,
        input_grad,
        moment4,
        moment5,
        new4,
        new5,
        copy4,
        copy5,
        bias_moment,
        bias_new,
    )


def solution(mesh):
    rows = P(("stream", "dp"), None)
    field = P(("stream", "dp"), None, None, None)
    return jax.shard_map(
        functools.partial(on_device, mesh.shape["dp"]),
        mesh=mesh,
        in_specs=(field, field, P(("stream", "dp")), rows, rows, rows, rows, rows, rows),
        out_specs=(field, field) + (rows,) * 8,
        check_vma=False,
    )
```

time: 1380 us -> 443 us (0.32)
  waiting for transfers between devices: 729 us -> 106 us
  local copies, waits for them, and re-layouts: 324 us -> 40.3 us
  starting transfers between devices: 1.44 us -> 144 us
  matrix products: 156 us -> 63.8 us
  blocking collectives: 82.7 us -> 0 us
  Pallas kernels: 0 us -> 30.5 us
  between operations: 16.4 us -> 2.44 us
    psum x5 -> x0, waiting for transfers between devices: 489 us -> none  [on_device(): gram4, gram5 = lax.psum((gram_of(iterate4), gram_of(iterate5)), 'dp')]
    reduce_scatter x2 -> x0, waiting for transfers between devices: 186 us -> none  [the longest x1 175 us: on_device(): lax.psum_scatter(whole4, 'dp', scatter_dimension=0, tiled=True)]
    slice x7 -> x15, local copies, waits for them, and re-layouts: 161 us -> 4.16 us  [the longest x6 1.92 us: scatter_sum(): two = self.fold(self.fold(parts[:, :, :, half:], 1, 1, kind), 1, 2, kind)]
    dot_general x36 -> x2, matrix products: 156 us -> 0.92 us  [gram_of(): lax.dot_general(low, low, (((0,), (0,)), ((), ())), preferred_element_typ...]
    ppermute x0 -> x94, starting transfers between devices: none -> 144 us  [the longest x47 75.3 us: fold(): got = lax.ppermute(out.astype(kind), 'dp', shift_pairs(self.dims, axis, j))]
    ppermute x0 -> x94, waiting for transfers between devices: none -> 106 us  [the longest x47 52.9 us: spread(): got.append(lax.ppermute(block, 'dp', shift_pairs(self.dims, axis, -j)))]
    reshape x7 -> x0, local copies, waits for them, and re-layouts: 90.2 us -> none  [the longest x2 62 us: fold_taps(): pieces = grads.reshape(count, side, side, 9, width)]
    conv_general_dilated x0 -> x10, matrix products: none -> 62.9 us  [the longest x2 25.5 us: weight_gradient(): lax.conv_general_dilated(field, delta, (1, 1), ((1, 1), (1, 1)), dimensio...]
  transfers between devices with their start and end apart: 10 -> 94, of which waited for: 10 -> 35; matrix products, arithmetic and copies ran while one was open for 32% -> 20% of each run, Pallas kernels for 0% -> 3%
where the time goes in v1:
time: 443 us; the launch traced here: 439 us
  starting transfers between devices  144 us (33%)
  waiting for transfers between devices  106 us (24%)
  matrix products  63.8 us (14%)
  other arithmetic  53.2 us (12%)
  local copies, waits for them, and re-layouts  40.3 us (9%)
  Pallas kernels  30.5 us (7%)
    ppermute x47, starting transfers between devices, fold(): got = lax.ppermute(out.astype(kind), 'dp', shift_pairs(self.dims, axis, j))  75.3 us
    ppermute x47, starting transfers between devices, spread(): got.append(lax.ppermute(block, 'dp', shift_pairs(self.dims, axis, -j)))  68.3 us
    ppermute x47, waiting for transfers between devices, spread(): got.append(lax.ppermute(block, 'dp', shift_pairs(self.dims, axis, -j)))  52.9 us
    ppermute x47, waiting for transfers between devices, fold(): got = lax.ppermute(out.astype(kind), 'dp', shift_pairs(self.dims, axis, j))  52.6 us
    pallas_call x2, Pallas kernels, newton(): pl.pallas_call(newton_kernel, out_shape=(jax.ShapeDtypeStruct(weight.shap...  30.5 us
    concatenate x18, other arithmetic, settle(): return jnp.roll(stack, self.place[axis], axis=at)  27 us
    conv_general_dilated x2, matrix products, weight_gradient(): lax.conv_general_dilated(field, delta, (1, 1), ((1, 1), (1, 1)), dimensio...  25.5 us
    conv_general_dilated x4, matrix products, convolve_back(): lax.conv_general_dilated(delta, weight.reshape(3, 3, -1, width)[::-1, ::-...  19.7 us
  transfers between devices with their start and end apart: 94, of which 35 were waited for; matrix products, arithmetic and copies ran while one was open for 20% of the time, Pallas kernels for 3%

profile of v1, /device:TPU:0, one launch (start us, length us, event | category | flops | bytes accessed | tf_op | source)
XLA Modules:
  0.0 439.5 jit_solution(12822322697660370555)
XLA Ops:
  1.5 4.0 collective-permute-start.15
  9.8 2.9 collective-permute-start.26
  19.3 2.1 collective-permute-done.17
  22.9 2.1 collective-permute-done.18
  26.4 3.4 collective-permute-done.1
  29.8 4.3 collective-permute-start.7
  34.2 4.1 collective-permute-start.9
  38.4 2.9 collective-permute-done.8
  42.4 3.4 collective-permute-start.20
  45.8 3.1 collective-permute-start.19
  52.6 6.1 %collective-permute-done.20 = bf16[288,256]{1,0:T(8,128)(2,1)S(1)} collective-permute-done((bf16[288,256]{1,0:T(8,128)(2,1)S(1)}, bf16[288,256]{1,0:T(8,128)(2,1)S(1)}, u32[]{:S(2)}, u32[]{:S(2)}) %collective-permute-start.20) | collective-permute-done | bytes 147488 | tf_op jit(solution)/shard_map/ppermute | solution.py:42
  62.4 5.7 %collective-permute-done.29 = bf16[4,144,256]{2,1,0:T(8,128)(2,1)S(1)} collective-permute-done((bf16[4,144,256]{2,1,0:T(8,128)(2,1)S(1)}, bf16[4,144,256]{2,1,0:T(8,128)(2,1)S(1)}, u32[]{:S(2)}, u32[]{:S(2)}) %collective-permute-start.29) | collective-permute-done | bytes 294944 | tf_op jit(solution)/shard_map/ppermute | solution.py:42
  69.7 2.6 collective-permute-done.31
  79.2 2.8 collective-permute-done.24
  86.2 11.1 %collective-permute-done.6 = bf16[2,4,144,256]{3,2,1,0:T(8,128)(2,1)S(1)} collective-permute-done((bf16[2,4,144,256]{3,2,1,0:T(8,128)(2,1)S(1)}, bf16[2,4,144,256]{3,2,1,0:T(8,128)(2,1)S(1)}, u32[]{:S(2)}, u32[]{:S(2)}) %collective-permute-start.6) | collective-permute-done | bytes 589856 | tf_op jit(solution)/shard_map/ppermute | solution.py:42
  99.5 10.3 %collective-permute-done.13 = bf16[2,4,144,256]{3,2,1,0:T(8,128)(2,1)S(1)} collective-permute-done((bf16[2,4,144,256]{3,2,1,0:T(8,128)(2,1)S(1)}, bf16[2,4,144,256]{3,2,1,0:T(8,128)(2,1)S(1)}, u32[]{:S(2)}, u32[]{:S(2)}) %collective-permute-start.13) | collective-permute-done | bytes 589856 | tf_op jit(solution)/shard_map/ppermute | solution.py:42
  110.5 3.4 fusion.32
  114.0 3.4 fusion.27
  119.2 2.8 fusion.24
  123.8 3.6 fusion.22
  127.5 2.3 fusion.20
  129.7 3.3 rev.15
  133.0 3.2 copy.63
  136.2 3.2 rev.14
  139.5 6.1 %fusion.193 = f32[8,13,13,256]{3,0,2,1:T(8,128)} fusion(bf16[8,13,13,512]{3,0,2,1:T(8,128)(2,1)S(1)} %copy-done, bf16[3,3,512,256]{3,2,1,0:T(8,128)(2,1)} %bitcast.423), kind=kOutput, calls=%fused_computation.445 | convolution fusion | flops 2871001088 | bytes 5128192 | tf_op jit(solution)/shard_map/conv_general_dilated | solution.py:109
  147.4 4.5 %fusion.192 = f32[8,13,13,256]{3,0,2,1:T(8,128)} fusion(bf16[8,13,13,512]{3,0,2,1:T(8,128)(2,1)S(1)} %copy-done, bf16[3,3,512,256]{3,2,1,0:T(8,128)(2,1)S(1)} %bitcast.425), kind=kOutput, calls=%fused_computation.444 | convolution fusion | flops 2871001088 | bytes 5128192 | tf_op jit(solution)/shard_map/conv_general_dilated | solution.py:109
  153.2 3.4 fusion.17
  158.3 3.1 fusion.14
  163.0 3.2 rev.13
  166.2 3.2 copy.73
  169.4 3.4 rev.12
  172.8 2.4 multiply_convert_fusion.1
  175.3 3.5 fusion.195
  178.9 3.4 fusion.194
  182.3 3.5 convert_reduce_fusion
  186.5 11.3 %fusion.197 = f32[3,3,512,512]{3,2,1,0:T(8,128)} fusion(bf16[8,13,13,512]{3,0,2,1:T(8,128)(2,1)} %copy-done.27, bf16[8,13,13,512]{3,0,2,1:T(8,128)(2,1)S(1)} %get-tuple-element.27), kind=kOutput, calls=%fused_computation.449 | convolution fusion | flops 5742002176 | bytes 12206080 | tf_op jit(solution)/shard_map/conv_general_dilated | solution.py:132
  197.8 3.4 fusion.56
  201.3 6.4 %convert_reduce_fusion.1 = (f32[512]{0:T(512)S(1)}, bf16[8,13,13,512]{3,0,2,1:T(8,128)(2,1)}) fusion(f32[512]{0:T(512)S(1)} %bitcast.476, f32[8,13,13,256]{3,0,2,1:T(8,128)S(1)} %copy-done.25, f32[8,13,13,256]{3,0,2,1:T(8,128)S(1)} %copy-done.26, f32[8,13,13,512]{3,0,2,1:T(8,128)S(1)} %fusion.56, bf16[3,3,512,256]{3,2,1,0:T(8,128)(2,1)S(1)} %copy-done.21, ...), kind=kOutput, calls=%fused_computation.53 | convolution fusion | flops 2888306176 | bytes 9977856 | tf_op jit(solution)/shard_map/conv_general_dilated | solution.py:121
  209.9 14.2 %fusion.196 = f32[3,3,512,512]{3,2,1,0:T(8,128)} fusion(bf16[8,13,13,512]{3,0,2,1:T(8,128)(2,1)S(1)} %copy-done, bf16[8,13,13,512]{3,0,2,1:T(8,128)(2,1)} %get-tuple-element.143), kind=kOutput, calls=%fused_computation.448 | convolution fusion | flops 5742002176 | bytes 12206080 | tf_op jit(solution)/shard_map/conv_general_dilated | solution.py:132
  224.2 5.0 %fusion.53 = f32[8,13,13,512]{3,0,2,1:T(8,128)} fusion(bf16[3,3,512,256]{3,2,1,0:T(8,128)(2,1)S(1)} %copy-done.20, bf16[8,13,13,512]{3,0,2,1:T(8,128)(2,1)S(1)} %copy-done.40), kind=kOutput, calls=%fused_computation.172 | convolution fusion | flops 2871001088 | bytes 5820416 | tf_op jit(solution)/shard_map/conv_general_dilated | solution.py:121
  242.3 4.9 %add_convert_fusion = bf16[8,13,13,512]{3,0,2,1:T(8,128)(2,1)} fusion(f32[8,13,13,512]{3,0,2,1:T(8,128)S(1)} %copy-done.39, bf16[3,3,512,256]{3,2,1,0:T(8,128)(2,1)S(1)} %copy-done.19, bf16[8,13,13,512]{3,0,2,1:T(8,128)(2,1)S(1)} %copy-done.41), kind=kOutput, calls=%fused_computation.54 | convolution fusion | flops 2872385536 | bytes 7204864 | tf_op jit(solution)/shard_map/conv_general_dilated | solution.py:121
  249.3 2.6 collective-permute-done.90
  251.9 4.4 collective-permute-start.91
  267.1 7.5 %collective-permute-done.47 = bf16[4,2,144,256]{3,2,0,1:T(8,128)(2,1)S(1)} collective-permute-done((bf16[4,2,144,256]{3,2,0,1:T(8,128)(2,1)S(1)}, bf16[4,2,144,256]{3,2,0,1:T(8,128)(2,1)S(1)}, u32[]{:S(2)}, u32[]{:S(2)}) %collective-permute-start.47) | collective-permute-done | bytes 589856 | tf_op jit(solution)/shard_map/ppermute | solution.py:73
  277.5 9.8 %collective-permute-done.40 = bf16[4,2,144,256]{3,2,0,1:T(8,128)(2,1)S(1)} collective-permute-done((bf16[4,2,144,256]{3,2,0,1:T(8,128)(2,1)S(1)}, bf16[4,2,144,256]{3,2,0,1:T(8,128)(2,1)S(1)}, u32[]{:S(2)}, u32[]{:S(2)}) %collective-permute-start.40) | collective-permute-done | bytes 589856 | tf_op jit(solution)/shard_map/ppermute | solution.py:73
  290.3 9.7 %collective-permute-done.33 = bf16[4,2,144,256]{3,2,0,1:T(8,128)(2,1)S(1)} collective-permute-done((bf16[4,2,144,256]{3,2,0,1:T(8,128)(2,1)S(1)}, bf16[4,2,144,256]{3,2,0,1:T(8,128)(2,1)S(1)}, u32[]{:S(2)}, u32[]{:S(2)}) %collective-permute-start.33) | collective-permute-done | bytes 589856 | tf_op jit(solution)/shard_map/ppermute | solution.py:73
  303.0 4.7 %collective-permute-done.55 = bf16[4,144,256]{2,1,0:T(8,128)(2,1)S(1)} collective-permute-done((bf16[4,144,256]{2,1,0:T(8,128)(2,1)S(1)}, bf16[4,144,256]{2,1,0:T(8,128)(2,1)S(1)}, u32[]{:S(2)}, u32[]{:S(2)}) %collective-permute-start.55) | collective-permute-done | bytes 294944 | tf_op jit(solution)/shard_map/ppermute | solution.py:73
  309.9 2.5 collective-permute-done.48
  316.8 2.4 collective-permute-start.60
  324.8 4.8 %collective-permute-done.59 = bf16[288,256]{1,0:T(8,128)(2,1)S(1)} collective-permute-done((bf16[288,256]{1,0:T(8,128)(2,1)S(1)}, bf16[288,256]{1,0:T(8,128)(2,1)S(1)}, u32[]{:S(2)}, u32[]{:S(2)}) %collective-permute-start.59) | collective-permute-done | bytes 147488 | tf_op jit(solution)/shard_map/ppermute | solution.py:73
  329.6 2.2 collective-permute-start.44
  331.8 6.8 %collective-permute-start.45 = (bf16[288,256]{1,0:T(8,128)(2,1)S(1)}, bf16[288,256]{1,0:T(8,128)(2,1)S(1)}, u32[]{:S(2)}, u32[]{:S(2)}) collective-permute-start(bf16[288,256]{1,0:T(8,128)(2,1)S(1)} %get-tuple-element.55), channel_id=1, source_target_pairs={{0,8},{1,9},{2,10},{3,11},{4,12},{5,13},{6,14},{7,15},{8,0},{9,1},... | collective-permute-start | bytes 442376 | tf_op jit(solution)/shard_map/ppermute | solution.py:73
  338.7 3.9 collective-permute-start.46
  345.2 3.4 collective-permute-start.38
  350.2 2.7 collective-permute-start.39
  354.7 3.2 collective-permute-done.38
  361.0 2.6 collective-permute-start.77
  372.5 3.6 collective-permute-start.79
  376.2 2.4 collective-permute-start.81
  378.8 2.5 collective-permute-start.66
  383.4 2.2 collective-permute-start.83
  389.1 2.6 collective-permute-start.68
  404.9 15.2 %shard_map.169 = (f32[288,512]{1,0:T(8,128)}, bf16[288,512]{1,0:T(8,128)(2,1)}) custom-call(f32[512,512]{1,0:T(8,128)S(1)} %maximum_maximum_fusion.1.gram_ref, f32[288,512]{1,0:T(8,128)S(1)} %get-tuple-element.28.update_ref, f32[288,512]{1,0:T(8,128)S(1)} %copy-done.2), custom_call_target="tpu_custom_call" | custom-call | flops 13421772800 | bytes 4194304 | tf_op jit(solution)/shard_map/pallas_call | solution.py:174
  423.9 15.3 %shard_map.168 = (f32[288,512]{1,0:T(8,128)}, bf16[288,512]{1,0:T(8,128)(2,1)}) custom-call(f32[512,512]{1,0:T(8,128)S(1)} %maximum_maximum_fusion.gram_ref, f32[288,512]{1,0:T(8,128)S(1)} %get-tuple-element.30.update_ref, f32[288,512]{1,0:T(8,128)S(1)} %copy-done.4), custom_call_target="tpu_custom_call" | custom-call | flops 13421772800 | bytes 4194304 | tf_op jit(solution)/shard_map/pallas_call | solution.py:174
  (405 shorter events, 138.7 us)
Async XLA Ops:
  1.5 14.0 %collective-permute-start.15 = (bf16[32,2]{0,1:T(2,128)(2,1)S(1)}, bf16[32,2]{0,1:T(2,128)(2,1)S(1)}, u32[]{:S(2)}, u32[]{:S(2)}) collective-permute-start(bf16[32,2]{0,1:T(2,128)(2,1)S(1)} %convert_element_type.305), channel_id=1, source_target_pairs={{0,8},{1,9},{2,10},{3,11},{4,12},{5,13},{6,14},{7,15},{8,0},{9,1},... | collective-permute-start | bytes 392 | tf_op jit(solution)/shard_map/ppermute | solution.py:42
  5.5 11.3 %collective-permute-start.14 = (bf16[32,2]{0,1:T(2,128)(2,1)S(1)}, bf16[32,2]{0,1:T(2,128)(2,1)S(1)}, u32[]{:S(2)}, u32[]{:S(2)}) collective-permute-start(bf16[32,2]{0,1:T(2,128)(2,1)S(1)} %convert_element_type.305), channel_id=1, source_target_pairs={{0,12},{1,13},{2,14},{3,15},{4,0},{5,1},{6,2},{7,3},{8,4},{9,5},{1... | collective-permute-start | bytes 392 | tf_op jit(solution)/shard_map/ppermute | solution.py:42
  6.9 10.8 %collective-permute-start.16 = (bf16[32,2]{0,1:T(2,128)(2,1)S(1)}, bf16[32,2]{0,1:T(2,128)(2,1)S(1)}, u32[]{:S(2)}, u32[]{:S(2)}) collective-permute-start(bf16[32,2]{0,1:T(2,128)(2,1)S(1)} %convert_element_type.305), channel_id=1, source_target_pairs={{0,4},{1,5},{2,6},{3,7},{4,8},{5,9},{6,10},{7,11},{8,12},{9,13},{1... | collective-permute-start | bytes 392 | tf_op jit(solution)/shard_map/ppermute | solution.py:42
  8.7 40.4 %collective-permute-start.27 = (bf16[288,256]{1,0:T(8,128)(2,1)S(1)}, bf16[288,256]{1,0:T(8,128)(2,1)S(1)}, u32[]{:S(2)}, u32[]{:S(2)}) collective-permute-start(bf16[288,256]{1,0:T(8,128)(2,1)S(1)} %get-tuple-element.103), channel_id=1, source_target_pairs={{0,8},{1,9},{2,10},{3,11},{4,12},{5,13},{6,14},{7,15},{8,0},{9,1},... | collective-permute-start | bytes 442376 | tf_op jit(solution)/shard_map/ppermute | solution.py:42
  9.8 39.6 %collective-permute-start.26 = (bf16[288,256]{1,0:T(8,128)(2,1)S(1)}, bf16[288,256]{1,0:T(8,128)(2,1)S(1)}, u32[]{:S(2)}, u32[]{:S(2)}) collective-permute-start(bf16[288,256]{1,0:T(8,128)(2,1)S(1)} %get-tuple-element.103), channel_id=1, source_target_pairs={{0,12},{1,13},{2,14},{3,15},{4,0},{5,1},{6,2},{7,3},{8,4},{9,5},{1... | collective-permute-start | bytes 442376 | tf_op jit(solution)/shard_map/ppermute | solution.py:42
  15.5 14.3 %collective-permute-start.1 = (bf16[288,256]{1,0:T(8,128)(2,1)S(1)}, bf16[288,256]{1,0:T(8,128)(2,1)S(1)}, u32[]{:S(2)}, u32[]{:S(2)}) collective-permute-start(bf16[288,256]{1,0:T(8,128)(2,1)S(1)} %get-tuple-element.108), channel_id=1, source_target_pairs={{0,8},{1,9},{2,10},{3,11},{4,12},{5,13},{6,14},{7,15},{8,0},{9,1},... | collective-permute-start | bytes 442376 | tf_op jit(solution)/shard_map/ppermute | solution.py:42
  16.8 13.0 %collective-permute-start = (bf16[288,256]{1,0:T(8,128)(2,1)S(1)}, bf16[288,256]{1,0:T(8,128)(2,1)S(1)}, u32[]{:S(2)}, u32[]{:S(2)}) collective-permute-start(bf16[288,256]{1,0:T(8,128)(2,1)S(1)} %get-tuple-element.108), channel_id=1, source_target_pairs={{0,12},{1,13},{2,14},{3,15},{4,0},{5,1},{6,2},{7,3},{8,4},{9,5},{1... | collective-permute-start | bytes 442376 | tf_op jit(solution)/shard_map/ppermute | solution.py:42
  25.1 9.1 %collective-permute-start.2 = (bf16[288,256]{1,0:T(8,128)(2,1)S(1)}, bf16[288,256]{1,0:T(8,128)(2,1)S(1)}, u32[]{:S(2)}, u32[]{:S(2)}) collective-permute-start(bf16[288,256]{1,0:T(8,128)(2,1)S(1)} %get-tuple-element.108), channel_id=1, source_target_pairs={{0,4},{1,5},{2,6},{3,7},{4,8},{5,9},{6,10},{7,11},{8,12},{9,13},{1... | collective-permute-start | bytes 442376 | tf_op jit(solution)/shard_map/ppermute | solution.py:42
  29.8 11.5 %collective-permute-start.8 = (bf16[288,256]{1,0:T(8,128)(2,1)S(1)}, bf16[288,256]{1,0:T(8,128)(2,1)S(1)}, u32[]{:S(2)}, u32[]{:S(2)}) collective-permute-start(bf16[288,256]{1,0:T(8,128)(2,1)S(1)} %get-tuple-element.107), channel_id=1, source_target_pairs={{0,8},{1,9},{2,10},{3,11},{4,12},{5,13},{6,14},{7,15},{8,0},{9,1},... | collective-permute-start | bytes 442376 | tf_op jit(solution)/shard_map/ppermute | solution.py:42
  29.8 12.6 %collective-permute-start.7 = (bf16[288,256]{1,0:T(8,128)(2,1)S(1)}, bf16[288,256]{1,0:T(8,128)(2,1)S(1)}, u32[]{:S(2)}, u32[]{:S(2)}) collective-permute-start(bf16[288,256]{1,0:T(8,128)(2,1)S(1)} %get-tuple-element.107), channel_id=1, source_target_pairs={{0,12},{1,13},{2,14},{3,15},{4,0},{5,1},{6,2},{7,3},{8,4},{9,5},{1... | collective-permute-start | bytes 442376 | tf_op jit(solution)/shard_map/ppermute | solution.py:42
  34.2 11.7 %collective-permute-start.9 = (bf16[288,256]{1,0:T(8,128)(2,1)S(1)}, bf16[288,256]{1,0:T(8,128)(2,1)S(1)}, u32[]{:S(2)}, u32[]{:S(2)}) collective-permute-start(bf16[288,256]{1,0:T(8,128)(2,1)S(1)} %get-tuple-element.107), channel_id=1, source_target_pairs={{0,4},{1,5},{2,6},{3,7},{4,8},{5,9},{6,10},{7,11},{8,12},{9,13},{1... | collective-permute-start | bytes 442376 | tf_op jit(solution)/shard_map/ppermute | solution.py:42
  41.3 9.7 %collective-permute-start.28 = (bf16[288,256]{1,0:T(8,128)(2,1)S(1)}, bf16[288,256]{1,0:T(8,128)(2,1)S(1)}, u32[]{:S(2)}, u32[]{:S(2)}) collective-permute-start(bf16[288,256]{1,0:T(8,128)(2,1)S(1)} %get-tuple-element.103), channel_id=1, source_target_pairs={{0,4},{1,5},{2,6},{3,7},{4,8},{5,9},{6,10},{7,11},{8,12},{9,13},{1... | collective-permute-start | bytes 442376 | tf_op jit(solution)/shard_map/ppermute | solution.py:42
  42.4 16.3 %collective-permute-start.20 = (bf16[288,256]{1,0:T(8,128)(2,1)S(1)}, bf16[288,256]{1,0:T(8,128)(2,1)S(1)}, u32[]{:S(2)}, u32[]{:S(2)}) collective-permute-start(bf16[288,256]{1,0:T(8,128)(2,1)S(1)} %get-tuple-element.104), channel_id=1, source_target_pairs={{0,8},{1,9},{2,10},{3,11},{4,12},{5,13},{6,14},{7,15},{8,0},{9,1},... | collective-permute-start | bytes 442376 | tf_op jit(solution)/shard_map/ppermute | solution.py:42
  45.8 14.4 %collective-permute-start.19 = (bf16[288,256]{1,0:T(8,128)(2,1)S(1)}, bf16[288,256]{1,0:T(8,128)(2,1)S(1)}, u32[]{:S(2)}, u32[]{:S(2)}) collective-permute-start(bf16[288,256]{1,0:T(8,128)(2,1)S(1)} %get-tuple-element.104), channel_id=1, source_target_pairs={{0,12},{1,13},{2,14},{3,15},{4,0},{5,1},{6,2},{7,3},{8,4},{9,5},{1... | collective-permute-start | bytes 442376 | tf_op jit(solution)/shard_map/ppermute | solution.py:42
  49.1 11.6 %collective-permute-start.21 = (bf16[288,256]{1,0:T(8,128)(2,1)S(1)}, bf16[288,256]{1,0:T(8,128)(2,1)S(1)}, u32[]{:S(2)}, u32[]{:S(2)}) collective-permute-start(bf16[288,256]{1,0:T(8,128)(2,1)S(1)} %get-tuple-element.104), channel_id=1, source_target_pairs={{0,4},{1,5},{2,6},{3,7},{4,8},{5,9},{6,10},{7,11},{8,12},{9,13},{1... | collective-permute-start | bytes 442376 | tf_op jit(solution)/shard_map/ppermute | solution.py:42
  49.4 25.2 %collective-permute-start.5 = (bf16[4,144,256]{2,1,0:T(8,128)(2,1)S(1)}, bf16[4,144,256]{2,1,0:T(8,128)(2,1)S(1)}, u32[]{:S(2)}, u32[]{:S(2)}) collective-permute-start(bf16[4,144,256]{2,1,0:T(8,128)(2,1)S(1)} %get-tuple-element.89), channel_id=1, source_target_pairs={{0,2},{1,3},{2,0},{3,1},{4,6},{5,7},{6,4},{7,5},{8,10},{9,11},{10,... | collective-permute-start | bytes 884744 | tf_op jit(solution)/shard_map/ppermute | solution.py:42
  51.0 25.2 %collective-permute-start.3 = (bf16[4,144,256]{2,1,0:T(8,128)(2,1)S(1)}, bf16[4,144,256]{2,1,0:T(8,128)(2,1)S(1)}, u32[]{:S(2)}, u32[]{:S(2)}) collective-permute-start(bf16[4,144,256]{2,1,0:T(8,128)(2,1)S(1)} %get-tuple-element.90), channel_id=1, source_target_pairs={{0,1},{1,0},{2,3},{3,2},{4,5},{5,4},{6,7},{7,6},{8,9},{9,8},{10,11... | collective-permute-start | bytes 884744 | tf_op jit(solution)/shard_map/ppermute | solution.py:42
  58.7 18.2 %collective-permute-start.12 = (bf16[4,144,256]{2,1,0:T(8,128)(2,1)S(1)}, bf16[4,144,256]{2,1,0:T(8,128)(2,1)S(1)}, u32[]{:S(2)}, u32[]{:S(2)}) collective-permute-start(bf16[4,144,256]{2,1,0:T(8,128)(2,1)S(1)} %get-tuple-element.97), channel_id=1, source_target_pairs={{0,2},{1,3},{2,0},{3,1},{4,6},{5,7},{6,4},{7,5},{8,10},{9,11},{10,... | collective-permute-start | bytes 884744 | tf_op jit(solution)/shard_map/ppermute | solution.py:42
  60.2 12.0 %collective-permute-start.31 = (bf16[4,144,256]{2,1,0:T(8,128)(2,1)S(1)}, bf16[4,144,256]{2,1,0:T(8,128)(2,1)S(1)}, u32[]{:S(2)}, u32[]{:S(2)}) collective-permute-start(bf16[4,144,256]{2,1,0:T(8,128)(2,1)S(1)} %get-tuple-element.81), channel_id=1, source_target_pairs={{0,2},{1,3},{2,0},{3,1},{4,6},{5,7},{6,4},{7,5},{8,10},{9,11},{10,... | collective-permute-start | bytes 884744 | tf_op jit(solution)/shard_map/ppermute | solution.py:42
  68.1 9.5 %collective-permute-start.10 = (bf16[4,144,256]{2,1,0:T(8,128)(2,1)S(1)}, bf16[4,144,256]{2,1,0:T(8,128)(2,1)S(1)}, u32[]{:S(2)}, u32[]{:S(2)}) collective-permute-start(bf16[4,144,256]{2,1,0:T(8,128)(2,1)S(1)} %get-tuple-element.98), channel_id=1, source_target_pairs={{0,1},{1,0},{2,3},{3,2},{4,5},{5,4},{6,7},{7,6},{8,9},{9,8},{10,11... | collective-permute-start | bytes 884744 | tf_op jit(solution)/shard_map/ppermute | solution.py:42
  72.2 9.8 %collective-permute-start.24 = (bf16[4,144,256]{2,1,0:T(8,128)(2,1)S(1)}, bf16[4,144,256]{2,1,0:T(8,128)(2,1)S(1)}, u32[]{:S(2)}, u32[]{:S(2)}) collective-permute-start(bf16[4,144,256]{2,1,0:T(8,128)(2,1)S(1)} %get-tuple-element.73), channel_id=1, source_target_pairs={{0,2},{1,3},{2,0},{3,1},{4,6},{5,7},{6,4},{7,5},{8,10},{9,11},{10,... | collective-permute-start | bytes 884744 | tf_op jit(solution)/shard_map/ppermute | solution.py:42
  74.6 9.9 %collective-permute-start.22 = (bf16[4,144,256]{2,1,0:T(8,128)(2,1)S(1)}, bf16[4,144,256]{2,1,0:T(8,128)(2,1)S(1)}, u32[]{:S(2)}, u32[]{:S(2)}) collective-permute-start(bf16[4,144,256]{2,1,0:T(8,128)(2,1)S(1)} %get-tuple-element.74), channel_id=1, source_target_pairs={{0,1},{1,0},{2,3},{3,2},{4,5},{5,4},{6,7},{7,6},{8,9},{9,8},{10,11... | collective-permute-start | bytes 884744 | tf_op jit(solution)/shard_map/ppermute | solution.py:42
  76.2 21.0 %collective-permute-start.6 = (bf16[2,4,144,256]{3,2,1,0:T(8,128)(2,1)S(1)}, bf16[2,4,144,256]{3,2,1,0:T(8,128)(2,1)S(1)}, u32[]{:S(2)}, u32[]{:S(2)}) collective-permute-start(bf16[2,4,144,256]{3,2,1,0:T(8,128)(2,1)S(1)} %get-tuple-element.86), channel_id=1, source_target_pairs={{0,1},{1,0},{2,3},{3,2},{4,5},{5,4},{6,7},{7,6},{8,9},{9,8},{10,11... | collective-permute-start | bytes 1769480 | tf_op jit(solution)/shard_map/ppermute | solution.py:42
  76.9 20.9 %collective-permute-start.4 = (bf16[2,4,144,256]{3,2,1,0:T(8,128)(2,1)S(1)}, bf16[2,4,144,256]{3,2,1,0:T(8,128)(2,1)S(1)}, u32[]{:S(2)}, u32[]{:S(2)}) collective-permute-start(bf16[2,4,144,256]{3,2,1,0:T(8,128)(2,1)S(1)} %get-tuple-element.92), channel_id=1, source_target_pairs={{0,2},{1,3},{2,0},{3,1},{4,6},{5,7},{6,4},{7,5},{8,10},{9,11},{10,... | collective-permute-start | bytes 1769480 | tf_op jit(solution)/shard_map/ppermute | solution.py:42
  77.6 32.3 %collective-permute-start.13 = (bf16[2,4,144,256]{3,2,1,0:T(8,128)(2,1)S(1)}, bf16[2,4,144,256]{3,2,1,0:T(8,128)(2,1)S(1)}, u32[]{:S(2)}, u32[]{:S(2)}) collective-permute-start(bf16[2,4,144,256]{3,2,1,0:T(8,128)(2,1)S(1)} %get-tuple-element.94), channel_id=1, source_target_pairs={{0,1},{1,0},{2,3},{3,2},{4,5},{5,4},{6,7},{7,6},{8,9},{9,8},{10,11... | collective-permute-start | bytes 1769480 | tf_op jit(solution)/shard_map/ppermute | solution.py:42
  82.0 31.9 %collective-permute-start.11 = (bf16[2,4,144,256]{3,2,1,0:T(8,128)(2,1)S(1)}, bf16[2,4,144,256]{3,2,1,0:T(8,128)(2,1)S(1)}, u32[]{:S(2)}, u32[]{:S(2)}) collective-permute-start(bf16[2,4,144,256]{3,2,1,0:T(8,128)(2,1)S(1)} %get-tuple-element.100), channel_id=1, source_target_pairs={{0,2},{1,3},{2,0},{3,1},{4,6},{5,7},{6,4},{7,5},{8,10},{9,11},{10,... | collective-permute-start | bytes 1769480 | tf_op jit(solution)/shard_map/ppermute | solution.py:42
  84.6 39.0 %collective-permute-start.25 = (bf16[2,4,144,256]{3,2,1,0:T(8,128)(2,1)S(1)}, bf16[2,4,144,256]{3,2,1,0:T(8,128)(2,1)S(1)}, u32[]{:S(2)}, u32[]{:S(2)}) collective-permute-start(bf16[2,4,144,256]{3,2,1,0:T(8,128)(2,1)S(1)} %get-tuple-element.70), channel_id=1, source_target_pairs={{0,1},{1,0},{2,3},{3,2},{4,5},{5,4},{6,7},{7,6},{8,9},{9,8},{10,11... | collective-permute-start | bytes 1769480 | tf_op jit(solution)/shard_map/ppermute | solution.py:42
  97.2 26.5 %collective-permute-start.23 = (bf16[2,4,144,256]{3,2,1,0:T(8,128)(2,1)S(1)}, bf16[2,4,144,256]{3,2,1,0:T(8,128)(2,1)S(1)}, u32[]{:S(2)}, u32[]{:S(2)}) collective-permute-start(bf16[2,4,144,256]{3,2,1,0:T(8,128)(2,1)S(1)} %get-tuple-element.76), channel_id=1, source_target_pairs={{0,2},{1,3},{2,0},{3,1},{4,6},{5,7},{6,4},{7,5},{8,10},{9,11},{10,... | collective-permute-start | bytes 1769480 | tf_op jit(solution)/shard_map/ppermute | solution.py:42
  97.9 47.8 %collective-permute-start.32 = (bf16[2,4,144,256]{3,2,1,0:T(8,128)(2,1)}, bf16[2,4,144,256]{3,2,1,0:T(8,128)(2,1)}, u32[]{:S(2)}, u32[]{:S(2)}) collective-permute-start(bf16[2,4,144,256]{3,2,1,0:T(8,128)(2,1)} %get-tuple-element.78), channel_id=1, source_target_pairs={{0,1},{1,0},{2,3},{3,2},{4,5},{5,4},{6,7},{7,6},{8,9},{9,8},{10,11... | collective-permute-start | bytes 1769480 | tf_op jit(solution)/shard_map/ppermute | solution.py:42
  109.9 42.1 %collective-permute-start.30 = (bf16[2,4,144,256]{3,2,1,0:T(8,128)(2,1)S(1)}, bf16[2,4,144,256]{3,2,1,0:T(8,128)(2,1)}, u32[]{:S(2)}, u32[]{:S(2)}) collective-permute-start(bf16[2,4,144,256]{3,2,1,0:T(8,128)(2,1)S(1)} %get-tuple-element.84), channel_id=1, source_target_pairs={{0,2},{1,3},{2,0},{3,1},{4,6},{5,7},{6,4},{7,5},{8,10},{9,11},{10,... | collective-permute-start | bytes 1769480 | tf_op jit(solution)/shard_map/ppermute | solution.py:42
  208.5 38.9 %collective-permute-start.89 = (f32[4,2,32,2]{2,1,0,3:T(2,128)}, f32[4,2,32,2]{2,1,0,3:T(2,128)}, u32[]{:S(2)}, u32[]{:S(2)}) collective-permute-start(f32[4,2,32,2]{2,1,0,3:T(2,128)} %bitcast.193), channel_id=1, source_target_pairs={{0,1},{1,0},{2,3},{3,2},{4,5},{5,4},{6,7},{7,6},{8,9},{9,8},{10,11... | collective-permute-start | bytes 6152 | tf_op jit(solution)/shard_map/ppermute | solution.py:73
  236.1 26.7 %collective-permute-start.54 = (bf16[4,2,144,256]{3,2,0,1:T(8,128)(2,1)}, bf16[4,2,144,256]{3,2,0,1:T(8,128)(2,1)}, u32[]{:S(2)}, u32[]{:S(2)}) collective-permute-start(bf16[4,2,144,256]{3,2,0,1:T(8,128)(2,1)} %fusion.64), channel_id=1, source_target_pairs={{0,1},{1,0},{2,3},{3,2},{4,5},{5,4},{6,7},{7,6},{8,9},{9,8},{10,11... | collective-permute-start | bytes 1769480 | tf_op jit(solution)/shard_map/ppermute | solution.py:73
  236.7 28.6 %collective-permute-start.56 = (bf16[4,2,144,256]{3,2,0,1:T(8,128)(2,1)}, bf16[4,2,144,256]{3,2,0,1:T(8,128)(2,1)}, u32[]{:S(2)}, u32[]{:S(2)}) collective-permute-start(bf16[4,2,144,256]{3,2,0,1:T(8,128)(2,1)} %fusion.65), channel_id=1, source_target_pairs={{0,2},{1,3},{2,0},{3,1},{4,6},{5,7},{6,4},{7,5},{8,10},{9,11},{10,... | collective-permute-start | bytes 1769480 | tf_op jit(solution)/shard_map/ppermute | solution.py:73
  258.3 16.3 %collective-permute-start.47 = (bf16[4,2,144,256]{3,2,0,1:T(8,128)(2,1)S(1)}, bf16[4,2,144,256]{3,2,0,1:T(8,128)(2,1)S(1)}, u32[]{:S(2)}, u32[]{:S(2)}) collective-permute-start(bf16[4,2,144,256]{3,2,0,1:T(8,128)(2,1)S(1)} %copy-done.30), channel_id=1, source_target_pairs={{0,1},{1,0},{2,3},{3,2},{4,5},{5,4},{6,7},{7,6},{8,9},{9,8},{10,11... | collective-permute-start | bytes 1769480 | tf_op jit(solution)/shard_map/ppermute | solution.py:73
  259.9 16.3 %collective-permute-start.49 = (bf16[4,2,144,256]{3,2,0,1:T(8,128)(2,1)S(1)}, bf16[4,2,144,256]{3,2,0,1:T(8,128)(2,1)S(1)}, u32[]{:S(2)}, u32[]{:S(2)}) collective-permute-start(bf16[4,2,144,256]{3,2,0,1:T(8,128)(2,1)S(1)} %copy-done.29), channel_id=1, source_target_pairs={{0,2},{1,3},{2,0},{3,1},{4,6},{5,7},{6,4},{7,5},{8,10},{9,11},{10,... | collective-permute-start | bytes 1769480 | tf_op jit(solution)/shard_map/ppermute | solution.py:73
  261.0 26.3 %collective-permute-start.40 = (bf16[4,2,144,256]{3,2,0,1:T(8,128)(2,1)S(1)}, bf16[4,2,144,256]{3,2,0,1:T(8,128)(2,1)S(1)}, u32[]{:S(2)}, u32[]{:S(2)}) collective-permute-start(bf16[4,2,144,256]{3,2,0,1:T(8,128)(2,1)S(1)} %fusion.60), channel_id=1, source_target_pairs={{0,1},{1,0},{2,3},{3,2},{4,5},{5,4},{6,7},{7,6},{8,9},{9,8},{10,11... | collective-permute-start | bytes 1769480 | tf_op jit(solution)/shard_map/ppermute | solution.py:73
  262.9 25.9 %collective-permute-start.42 = (bf16[4,2,144,256]{3,2,0,1:T(8,128)(2,1)S(1)}, bf16[4,2,144,256]{3,2,0,1:T(8,128)(2,1)S(1)}, u32[]{:S(2)}, u32[]{:S(2)}) collective-permute-start(bf16[4,2,144,256]{3,2,0,1:T(8,128)(2,1)S(1)} %fusion.61), channel_id=1, source_target_pairs={{0,2},{1,3},{2,0},{3,1},{4,6},{5,7},{6,4},{7,5},{8,10},{9,11},{10,... | collective-permute-start | bytes 1769480 | tf_op jit(solution)/shard_map/ppermute | solution.py:73
  265.3 34.7 %collective-permute-start.33 = (bf16[4,2,144,256]{3,2,0,1:T(8,128)(2,1)S(1)}, bf16[4,2,144,256]{3,2,0,1:T(8,128)(2,1)S(1)}, u32[]{:S(2)}, u32[]{:S(2)}) collective-permute-start(bf16[4,2,144,256]{3,2,0,1:T(8,128)(2,1)S(1)} %fusion.58), channel_id=1, source_target_pairs={{0,1},{1,0},{2,3},{3,2},{4,5},{5,4},{6,7},{7,6},{8,9},{9,8},{10,11... | collective-permute-start | bytes 1769480 | tf_op jit(solution)/shard_map/ppermute | solution.py:73
  274.7 26.8 %collective-permute-start.35 = (bf16[4,2,144,256]{3,2,0,1:T(8,128)(2,1)S(1)}, bf16[4,2,144,256]{3,2,0,1:T(8,128)(2,1)S(1)}, u32[]{:S(2)}, u32[]{:S(2)}) collective-permute-start(bf16[4,2,144,256]{3,2,0,1:T(8,128)(2,1)S(1)} %fusion.59), channel_id=1, source_target_pairs={{0,2},{1,3},{2,0},{3,1},{4,6},{5,7},{6,4},{7,5},{8,10},{9,11},{10,... | collective-permute-start | bytes 1769480 | tf_op jit(solution)/shard_map/ppermute | solution.py:73
  276.1 31.6 %collective-permute-start.55 = (bf16[4,144,256]{2,1,0:T(8,128)(2,1)S(1)}, bf16[4,144,256]{2,1,0:T(8,128)(2,1)S(1)}, u32[]{:S(2)}, u32[]{:S(2)}) collective-permute-start(bf16[4,144,256]{2,1,0:T(8,128)(2,1)S(1)} %fusion.72), channel_id=1, source_target_pairs={{0,2},{1,3},{2,0},{3,1},{4,6},{5,7},{6,4},{7,5},{8,10},{9,11},{10,... | collective-permute-start | bytes 884744 | tf_op jit(solution)/shard_map/ppermute | solution.py:73
  287.3 22.0 %collective-permute-start.57 = (bf16[4,144,256]{2,1,0:T(8,128)(2,1)S(1)}, bf16[4,144,256]{2,1,0:T(8,128)(2,1)S(1)}, u32[]{:S(2)}, u32[]{:S(2)}) collective-permute-start(bf16[4,144,256]{2,1,0:T(8,128)(2,1)S(1)} %fusion.73), channel_id=1, source_target_pairs={{0,1},{1,0},{2,3},{3,2},{4,5},{5,4},{6,7},{7,6},{8,9},{9,8},{10,11... | collective-permute-start | bytes 884744 | tf_op jit(solution)/shard_map/ppermute | solution.py:73
  288.8 23.6 %collective-permute-start.48 = (bf16[4,144,256]{2,1,0:T(8,128)(2,1)S(1)}, bf16[4,144,256]{2,1,0:T(8,128)(2,1)S(1)}, u32[]{:S(2)}, u32[]{:S(2)}) collective-permute-start(bf16[4,144,256]{2,1,0:T(8,128)(2,1)S(1)} %fusion.70), channel_id=1, source_target_pairs={{0,2},{1,3},{2,0},{3,1},{4,6},{5,7},{6,4},{7,5},{8,10},{9,11},{10,... | collective-permute-start | bytes 884744 | tf_op jit(solution)/shard_map/ppermute | solution.py:73
  299.9 14.1 %collective-permute-start.50 = (bf16[4,144,256]{2,1,0:T(8,128)(2,1)S(1)}, bf16[4,144,256]{2,1,0:T(8,128)(2,1)S(1)}, u32[]{:S(2)}, u32[]{:S(2)}) collective-permute-start(bf16[4,144,256]{2,1,0:T(8,128)(2,1)S(1)} %fusion.71), channel_id=1, source_target_pairs={{0,1},{1,0},{2,3},{3,2},{4,5},{5,4},{6,7},{7,6},{8,9},{9,8},{10,11... | collective-permute-start | bytes 884744 | tf_op jit(solution)/shard_map/ppermute | solution.py:73
  301.4 14.1 %collective-permute-start.41 = (bf16[4,144,256]{2,1,0:T(8,128)(2,1)S(1)}, bf16[4,144,256]{2,1,0:T(8,128)(2,1)S(1)}, u32[]{:S(2)}, u32[]{:S(2)}) collective-permute-start(bf16[4,144,256]{2,1,0:T(8,128)(2,1)S(1)} %fusion.68), channel_id=1, source_target_pairs={{0,2},{1,3},{2,0},{3,1},{4,6},{5,7},{6,4},{7,5},{8,10},{9,11},{10,... | collective-permute-start | bytes 884744 | tf_op jit(solution)/shard_map/ppermute | solution.py:73
  307.7 9.1 %collective-permute-start.43 = (bf16[4,144,256]{2,1,0:T(8,128)(2,1)S(1)}, bf16[4,144,256]{2,1,0:T(8,128)(2,1)S(1)}, u32[]{:S(2)}, u32[]{:S(2)}) collective-permute-start(bf16[4,144,256]{2,1,0:T(8,128)(2,1)S(1)} %fusion.69), channel_id=1, source_target_pairs={{0,1},{1,0},{2,3},{3,2},{4,5},{5,4},{6,7},{7,6},{8,9},{9,8},{10,11... | collective-permute-start | bytes 884744 | tf_op jit(solution)/shard_map/ppermute | solution.py:73
  309.3 10.0 %collective-permute-start.34 = (bf16[4,144,256]{2,1,0:T(8,128)(2,1)S(1)}, bf16[4,144,256]{2,1,0:T(8,128)(2,1)S(1)}, u32[]{:S(2)}, u32[]{:S(2)}) collective-permute-start(bf16[4,144,256]{2,1,0:T(8,128)(2,1)S(1)} %fusion.66), channel_id=1, source_target_pairs={{0,2},{1,3},{2,0},{3,1},{4,6},{5,7},{6,4},{7,5},{8,10},{9,11},{10,... | collective-permute-start | bytes 884744 | tf_op jit(solution)/shard_map/ppermute | solution.py:73
  314.0 8.8 %collective-permute-start.58 = (bf16[288,256]{1,0:T(8,128)(2,1)S(1)}, bf16[288,256]{1,0:T(8,128)(2,1)S(1)}, u32[]{:S(2)}, u32[]{:S(2)}) collective-permute-start(bf16[288,256]{1,0:T(8,128)(2,1)S(1)} %get-tuple-element.48), channel_id=1, source_target_pairs={{0,4},{1,5},{2,6},{3,7},{4,8},{5,9},{6,10},{7,11},{8,12},{9,13},{1... | collective-permute-start | bytes 442376 | tf_op jit(solution)/shard_map/ppermute | solution.py:73
  315.6 14.1 %collective-permute-start.59 = (bf16[288,256]{1,0:T(8,128)(2,1)S(1)}, bf16[288,256]{1,0:T(8,128)(2,1)S(1)}, u32[]{:S(2)}, u32[]{:S(2)}) collective-permute-start(bf16[288,256]{1,0:T(8,128)(2,1)S(1)} %get-tuple-element.49), channel_id=1, source_target_pairs={{0,8},{1,9},{2,10},{3,11},{4,12},{5,13},{6,14},{7,15},{8,0},{9,1},... | collective-permute-start | bytes 442376 | tf_op jit(solution)/shard_map/ppermute | solution.py:73
  316.8 15.0 %collective-permute-start.60 = (bf16[288,256]{1,0:T(8,128)(2,1)S(1)}, bf16[288,256]{1,0:T(8,128)(2,1)S(1)}, u32[]{:S(2)}, u32[]{:S(2)}) collective-permute-start(bf16[288,256]{1,0:T(8,128)(2,1)S(1)} %get-tuple-element.50), channel_id=1, source_target_pairs={{0,12},{1,13},{2,14},{3,15},{4,0},{5,1},{6,2},{7,3},{8,4},{9,5},{1... | collective-permute-start | bytes 442376 | tf_op jit(solution)/shard_map/ppermute | solution.py:73
  319.3 19.4 %collective-permute-start.51 = (bf16[288,256]{1,0:T(8,128)(2,1)S(1)}, bf16[288,256]{1,0:T(8,128)(2,1)S(1)}, u32[]{:S(2)}, u32[]{:S(2)}) collective-permute-start(bf16[288,256]{1,0:T(8,128)(2,1)S(1)} %get-tuple-element.45), channel_id=1, source_target_pairs={{0,4},{1,5},{2,6},{3,7},{4,8},{5,9},{6,10},{7,11},{8,12},{9,13},{1... | collective-permute-start | bytes 442376 | tf_op jit(solution)/shard_map/ppermute | solution.py:73
  319.9 23.7 %collective-permute-start.52 = (bf16[288,256]{1,0:T(8,128)(2,1)S(1)}, bf16[288,256]{1,0:T(8,128)(2,1)S(1)}, u32[]{:S(2)}, u32[]{:S(2)}) collective-permute-start(bf16[288,256]{1,0:T(8,128)(2,1)S(1)} %get-tuple-element.46), channel_id=1, source_target_pairs={{0,8},{1,9},{2,10},{3,11},{4,12},{5,13},{6,14},{7,15},{8,0},{9,1},... | collective-permute-start | bytes 442376 | tf_op jit(solution)/shard_map/ppermute | solution.py:73
  322.9 22.3 %collective-permute-start.53 = (bf16[288,256]{1,0:T(8,128)(2,1)S(1)}, bf16[288,256]{1,0:T(8,128)(2,1)S(1)}, u32[]{:S(2)}, u32[]{:S(2)}) collective-permute-start(bf16[288,256]{1,0:T(8,128)(2,1)S(1)} %get-tuple-element.47), channel_id=1, source_target_pairs={{0,12},{1,13},{2,14},{3,15},{4,0},{5,1},{6,2},{7,3},{8,4},{9,5},{1... | collective-permute-start | bytes 442376 | tf_op jit(solution)/shard_map/ppermute | solution.py:73
  329.6 20.5 %collective-permute-start.44 = (bf16[288,256]{1,0:T(8,128)(2,1)S(1)}, bf16[288,256]{1,0:T(8,128)(2,1)S(1)}, u32[]{:S(2)}, u32[]{:S(2)}) collective-permute-start(bf16[288,256]{1,0:T(8,128)(2,1)S(1)} %get-tuple-element.54), channel_id=1, source_target_pairs={{0,4},{1,5},{2,6},{3,7},{4,8},{5,9},{6,10},{7,11},{8,12},{9,13},{1... | collective-permute-start | bytes 442376 | tf_op jit(solution)/shard_map/ppermute | solution.py:73
  331.8 22.8 %collective-permute-start.45 = (bf16[288,256]{1,0:T(8,128)(2,1)S(1)}, bf16[288,256]{1,0:T(8,128)(2,1)S(1)}, u32[]{:S(2)}, u32[]{:S(2)}) collective-permute-start(bf16[288,256]{1,0:T(8,128)(2,1)S(1)} %get-tuple-element.55), channel_id=1, source_target_pairs={{0,8},{1,9},{2,10},{3,11},{4,12},{5,13},{6,14},{7,15},{8,0},{9,1},... | collective-permute-start | bytes 442376 | tf_op jit(solution)/shard_map/ppermute | solution.py:73
  338.7 15.9 %collective-permute-start.46 = (bf16[288,256]{1,0:T(8,128)(2,1)S(1)}, bf16[288,256]{1,0:T(8,128)(2,1)S(1)}, u32[]{:S(2)}, u32[]{:S(2)}) collective-permute-start(bf16[288,256]{1,0:T(8,128)(2,1)S(1)} %get-tuple-element.56), channel_id=1, source_target_pairs={{0,12},{1,13},{2,14},{3,15},{4,0},{5,1},{6,2},{7,3},{8,4},{9,5},{1... | collective-permute-start | bytes 442376 | tf_op jit(solution)/shard_map/ppermute | solution.py:73
  343.6 11.1 %collective-permute-start.37 = (bf16[288,256]{1,0:T(8,128)(2,1)S(1)}, bf16[288,256]{1,0:T(8,128)(2,1)S(1)}, u32[]{:S(2)}, u32[]{:S(2)}) collective-permute-start(bf16[288,256]{1,0:T(8,128)(2,1)S(1)} %get-tuple-element.51), channel_id=1, source_target_pairs={{0,4},{1,5},{2,6},{3,7},{4,8},{5,9},{6,10},{7,11},{8,12},{9,13},{1... | collective-permute-start | bytes 442376 | tf_op jit(solution)/shard_map/ppermute | solution.py:73
  345.2 12.8 %collective-permute-start.38 = (bf16[288,256]{1,0:T(8,128)(2,1)S(1)}, bf16[288,256]{1,0:T(8,128)(2,1)S(1)}, u32[]{:S(2)}, u32[]{:S(2)}) collective-permute-start(bf16[288,256]{1,0:T(8,128)(2,1)S(1)} %get-tuple-element.52), channel_id=1, source_target_pairs={{0,8},{1,9},{2,10},{3,11},{4,12},{5,13},{6,14},{7,15},{8,0},{9,1},... | collective-permute-start | bytes 442376 | tf_op jit(solution)/shard_map/ppermute | solution.py:73
  369.5 9.1 %collective-permute-start.62 = (f32[4,24,256]{2,1,0:T(8,128)S(1)}, f32[4,24,256]{2,1,0:T(8,128)S(1)}, u32[]{:S(2)}, u32[]{:S(2)}) collective-permute-start(f32[4,24,256]{2,1,0:T(8,128)S(1)} %dynamic-slice_bitcast_fusion.7), channel_id=1, source_target_pairs={{0,2},{1,3},{2,0},{3,1},{4,6},{5,7},{6,4},{7,5},{8,10},{9,11},{10,... | collective-permute-start | bytes 294920 | tf_op jit(solution)/shard_map/ppermute | solution.py:73
  370.0 8.6 %collective-permute-start.64 = (f32[4,24,256]{2,1,0:T(8,128)S(1)}, f32[4,24,256]{2,1,0:T(8,128)S(1)}, u32[]{:S(2)}, u32[]{:S(2)}) collective-permute-start(f32[4,24,256]{2,1,0:T(8,128)S(1)} %dynamic-slice_bitcast_fusion.6), channel_id=1, source_target_pairs={{0,1},{1,0},{2,3},{3,2},{4,5},{5,4},{6,7},{7,6},{8,9},{9,8},{10,11... | collective-permute-start | bytes 294920 | tf_op jit(solution)/shard_map/ppermute | solution.py:73
  372.5 8.7 %collective-permute-start.79 = (f32[48,256]{1,0:T(8,128)S(1)}, f32[48,256]{1,0:T(8,128)S(1)}, u32[]{:S(2)}, u32[]{:S(2)}) collective-permute-start(f32[48,256]{1,0:T(8,128)S(1)} %get-tuple-element.117), channel_id=1, source_target_pairs={{0,4},{1,5},{2,6},{3,7},{4,8},{5,9},{6,10},{7,11},{8,12},{9,13},{1... | collective-permute-start | bytes 147464 | tf_op jit(solution)/shard_map/ppermute | solution.py:73
  378.8 8.9 %collective-permute-start.66 = (f32[48,256]{1,0:T(8,128)S(1)}, f32[48,256]{1,0:T(8,128)S(1)}, u32[]{:S(2)}, u32[]{:S(2)}) collective-permute-start(f32[48,256]{1,0:T(8,128)S(1)} %get-tuple-element.129), channel_id=1, source_target_pairs={{0,8},{1,9},{2,10},{3,11},{4,12},{5,13},{6,14},{7,15},{8,0},{9,1},... | collective-permute-start | bytes 147464 | tf_op jit(solution)/shard_map/ppermute | solution.py:73
  383.4 8.3 %collective-permute-start.83 = (f32[48,256]{1,0:T(8,128)S(1)}, f32[48,256]{1,0:T(8,128)S(1)}, u32[]{:S(2)}, u32[]{:S(2)}) collective-permute-start(f32[48,256]{1,0:T(8,128)S(1)} %fusion.140), channel_id=1, source_target_pairs={{0,8},{1,9},{2,10},{3,11},{4,12},{5,13},{6,14},{7,15},{8,0},{9,1},... | collective-permute-start | bytes 147464 | tf_op jit(solution)/shard_map/ppermute | solution.py:42
  399.7 20.4 %collective-permute-start.74 = (f32[2,4,24,256]{3,2,0,1:T(8,128)}, f32[2,4,24,256]{3,2,0,1:T(8,128)}, u32[]{:S(2)}, u32[]{:S(2)}) collective-permute-start(f32[2,4,24,256]{3,2,0,1:T(8,128)} %get-tuple-element.121), channel_id=1, source_target_pairs={{0,1},{1,0},{2,3},{3,2},{4,5},{5,4},{6,7},{7,6},{8,9},{9,8},{10,11... | collective-permute-start | bytes 589832 | tf_op jit(solution)/shard_map/ppermute | solution.py:42
  401.5 19.6 %collective-permute-start.72 = (f32[2,4,24,256]{3,2,1,0:T(8,128)}, f32[2,4,24,256]{3,2,1,0:T(8,128)}, u32[]{:S(2)}, u32[]{:S(2)}) collective-permute-start(f32[2,4,24,256]{3,2,1,0:T(8,128)} %get-tuple-element.127), channel_id=1, source_target_pairs={{0,2},{1,3},{2,0},{3,1},{4,6},{5,7},{6,4},{7,5},{8,10},{9,11},{10,... | collective-permute-start | bytes 589832 | tf_op jit(solution)/shard_map/ppermute | solution.py:42
  (76 other events, 782.0 us)
